TPU v7x, 32 devices: a whole 2x2x4 slice. The times are simulated.
32 devices in a mesh: groups: 2 (over y), tiles: 4 (over z), chan: 2 (over x), sub: 2 (over core).
Axes of the slice: x: 2, y: 2, z: 4, core: 2. Of those that a mesh axis runs over, the one named last changes fastest.
Arguments:
- features: bfloat16 [128, 256, 256], P(('groups', 'tiles', 'sub'), 'chan'), parts along dimension 0, may hold values from -6 to 6
- cotangent: bfloat16 [128, 256, 256], P(('groups', 'tiles', 'sub'), 'chan'), parts along dimension 0, may hold values from -6 to 6
- down_factor: bfloat16 [2, 256, 64], P(None, 'chan'), may hold values from -0.375 to 0.375
- core_kernel: bfloat16 [2, 9, 64, 64], replicated, may hold values from -0.25 to 0.25
- up_factor: bfloat16 [2, 256, 64], P(None, 'chan'), may hold values from -0.75 to 0.75
- tile_count: int32 [16], P(('groups', 'tiles', 'sub')), parts along dimension 0, may hold values from 4 to 8, as said below
- neighbour_owner: int32 [128, 8], P(('groups', 'tiles', 'sub')), parts along dimension 0, may hold values from -1 to 7, as said below
- neighbour_slot: int32 [128, 8], P(('groups', 'tiles', 'sub')), parts along dimension 0, may hold values from -1 to 7, as said below
Outputs:
- input_gradient: bfloat16 [128, 256, 256], P(('groups', 'tiles', 'sub'), 'chan'), parts along dimension 0
- down_gradient: float32 [4, 256, 64], P('groups', 'chan'), parts along dimension 0
- core_gradient: float32 [4, 9, 64, 64], P('groups', None, 'chan'), parts along dimension 0
- up_gradient: float32 [4, 256, 64], P('groups', 'chan'), parts along dimension 0
There are 2 independent parts, one for each index of `groups`. A program takes and returns all parts, laid end to end along the dimension named above; an argument that names none is the same for every part. Nothing has to cross between parts.
Inputs may be any that keep to these rules, and one draw needn't show every extreme that they name: `tile_count`: every count is even; some device holds exactly 8 live tiles and some exactly 4. `neighbour_owner`: -1 where the slot is not live or no tissue tile lies in that direction. Otherwise the owner is the slot's own device or the device just before or after it along the owners, and the named slot is live there. Neighbourhood is mutual: if tile h lies in some direction of tile g, then g lies in the opposite direction of h. `neighbour_slot`: -1 exactly where neighbour_owner is -1.
All inputs are finite; a program needn't handle non-finite values.
Results may differ from a plain program's by a relative error of at most 0.014.
Values may be sent and summed in bfloat16 or wider, within the bound.
A program may use at most 64 MiB of HBM per device.

v0:
```python
import jax
import jax.numpy as jnp
from jax import lax
from jax.sharding import PartitionSpec as P

TILE = 16
LAYERS = 2
EDGE_ROWS = [1, 6, 3, 4]
EDGE_PIECES = [1, 0, 3, 2]
CORNER_ROWS = [0, 2, 5, 7]
CORNER_PIECES = [3, 2, 1, 0]


def padded_2(cells, sides, width):
    for axis, dim in sides:
        count = lax.axis_size(axis)
        ends = count - 1
        head = lax.slice_in_dim(cells, 0, width, axis=dim)
        tail = lax.slice_in_dim(cells, cells.shape[dim] - width, cells.shape[dim], axis=dim)
        cells = jnp.concatenate(
            [
                lax.ppermute(tail, axis, [(i, (i + 1) % count) for i in range(ends)]),
                cells,
                lax.ppermute(head, axis, [((i + 1) % count, i) for i in range(ends)]),
            ],
            axis=dim,
        )
    return cells


def cycle_of(squares):
    edge_cells = jnp.concatenate(
        [squares[:, :, 0, :], squares[:, :, -1, :], squares[:, :, :, 0], squares[:, :, :, -1]],
        axis=2,
    )
    corners = jnp.stack(
        [squares[:, :, 0, 0], squares[:, :, 0, -1], squares[:, :, -1, 0], squares[:, :, -1, -1]],
        axis=2,
    )
    return jnp.concatenate([edge_cells, corners], axis=2)


def assemble(squares, side_cells, corner_cells):
    top_row = jnp.concatenate(
        [corner_cells[0][:, :, None], side_cells[0], corner_cells[1][:, :, None]], axis=2
    )
    bottom_row = jnp.concatenate(
        [corner_cells[2][:, :, None], side_cells[1], corner_cells[3][:, :, None]], axis=2
    )
    middle = jnp.concatenate(
        [side_cells[2][:, :, :, None], squares, side_cells[3][:, :, :, None]], axis=3
    )
    return jnp.concatenate([top_row[:, :, None, :], middle, bottom_row[:, :, None, :]], axis=2)


def selectors(neighbour_owner, neighbour_slot, device_here, slot_total):
    local_row = (neighbour_owner - device_here + 1) * slot_total + neighbour_slot
    columns = jnp.arange(3 * slot_total)
    matched = (local_row[:, :, None] == columns[None, None, :]) & (neighbour_owner[:, :, None] >= 0)
    return matched.astype(jnp.bfloat16)


def place_border(flat_cells, extended, chooser):
    squares = flat_cells.reshape(flat_cells.shape[0], flat_cells.shape[1], TILE, TILE)
    nearest = jnp.einsum(
        "uvd,dck->uvck",
        jnp.stack([chooser[:, row] for row in EDGE_ROWS], axis=1),
        extended[:, :, : 4 * TILE],
        preferred_element_type=jnp.float32,
    ).astype(jnp.bfloat16)
    diagonal = jnp.einsum(
        "uvd,dck->uvck",
        jnp.stack([chooser[:, row] for row in CORNER_ROWS], axis=1),
        extended[:, :, 4 * TILE :],
        preferred_element_type=jnp.float32,
    ).astype(jnp.bfloat16)
    side_cells = [
        nearest[:, which_side, :, piece_index * TILE : (piece_index + 1) * TILE]
        for which_side, piece_index in enumerate(EDGE_PIECES)
    ]
    corner_cells = [
        diagonal[:, which_side, :, piece_index]
        for which_side, piece_index in enumerate(CORNER_PIECES)
    ]
    return assemble(squares, side_cells, corner_cells)


def window(padded, shift_rows, shift_cols):
    section = padded[:, :, shift_rows : shift_rows + TILE, shift_cols : shift_cols + TILE]
    return section.reshape(section.shape[0], section.shape[1], TILE * TILE)


def stacked_windows(padded, flipped):
    if flipped:
        return jnp.stack(
            [window(padded, 2 - offset // 3, 2 - offset % 3) for offset in range(9)], axis=0
        )
    return jnp.stack([window(padded, offset // 3, offset % 3) for offset in range(9)], axis=0)


def forward_conv(windows, kernel):
    return jnp.einsum("tsr,turq->usq", kernel, windows, preferred_element_type=jnp.float32)


def backward_conv(padded, kernel):
    return jnp.einsum(
        "tsr,tusq->urq", kernel, stacked_windows(padded, True), preferred_element_type=jnp.float32
    )


def core_gradient_of(gradient, windows):
    return jnp.einsum("usq,turq->tsr", gradient, windows, preferred_element_type=jnp.float32)


def blocked_product(factor, data, members):
    width = factor.shape[0] // members
    running = jnp.zeros((data.shape[0], factor.shape[1], data.shape[2]), jnp.float32)
    for member in range(members):
        partial_value = jnp.einsum(
            "cr,ucq->urq",
            factor[member * width : (member + 1) * width],
            data[:, member * width : (member + 1) * width],
            preferred_element_type=jnp.float32,
        )
        running = running + lax.optimization_barrier(partial_value.astype(jnp.bfloat16)).astype(
            jnp.float32
        )
    return running.astype(jnp.bfloat16)


def settle(down_part, core_part, up_part):
    return (down_part, core_part, up_part)


def whole_tiles(
    features,
    cotangent,
    down_factor,
    core_kernel,
    up_factor,
    tile_count,
    neighbour_owner,
    neighbour_slot,
):
    slot_total = features.shape[0]
    members = lax.axis_size("chan")
    rows_here = slot_total // members
    device_here = lax.axis_index(("tiles", "sub"))
    first_slot = lax.axis_index("chan") * rows_here
    hidden, upstream = (
        lax.all_to_all(features, "chan", split_axis=0, concat_axis=1, tiled=True),
        lax.all_to_all(cotangent, "chan", split_axis=0, concat_axis=1, tiled=True),
    )
    alive = (first_slot + jnp.arange(rows_here) < tile_count[0]).astype(jnp.bfloat16)
    hidden = hidden * alive[:, None, None]
    upstream = upstream * alive[:, None, None]
    down_whole, up_whole = (
        lax.all_gather(down_factor, "chan", axis=1, tiled=True),
        lax.all_gather(up_factor, "chan", axis=1, tiled=True),
    )
    near_owner = lax.dynamic_slice_in_dim(neighbour_owner, first_slot, rows_here, 0)
    near_slot = lax.dynamic_slice_in_dim(neighbour_slot, first_slot, rows_here, 0)
    chooser = selectors(near_owner, near_slot, device_here, slot_total)

    def padded_of(cells):
        border = cycle_of(cells.reshape(rows_here, cells.shape[1], TILE, TILE))
        owner_cycle = lax.all_gather(border, "chan", axis=0, tiled=True)
        extended = padded_2(owner_cycle, ((("tiles", "sub"), 0),), slot_total)
        return place_border(cells, extended, chooser)

    saved_layers = []
    for layer_index in range(LAYERS):
        activations = blocked_product(down_whole[layer_index], hidden, members)
        windows = stacked_windows(padded_of(activations), False)
        mixed = forward_conv(windows, core_kernel[layer_index]).astype(jnp.bfloat16)
        preact = jnp.einsum(
            "cs,usq->ucq", up_whole[layer_index], mixed, preferred_element_type=jnp.float32
        )
        saved_layers.append((hidden, windows, mixed, preact))
        hidden = (hidden.astype(jnp.float32) + jax.nn.silu(preact)).astype(jnp.bfloat16)
    down_list = [None] * LAYERS
    core_list = [None] * LAYERS
    up_list = [None] * LAYERS
    for layer_index in reversed(range(LAYERS)):
        hidden, windows, mixed, preact = saved_layers[layer_index]
        squashed = jax.nn.sigmoid(preact)
        pre_gradient = (
            upstream.astype(jnp.float32) * squashed * (1.0 + preact * (1.0 - squashed))
        ).astype(jnp.bfloat16)
        up_part = jnp.einsum("ucq,usq->cs", pre_gradient, mixed, preferred_element_type=jnp.float32)
        mixed_gradient = blocked_product(up_whole[layer_index], pre_gradient, members)
        core_part = core_gradient_of(mixed_gradient, windows)
        gradient_padded = padded_of(mixed_gradient)
        act_gradient = backward_conv(gradient_padded, core_kernel[layer_index]).astype(jnp.bfloat16)
        down_part = jnp.einsum(
            "ucq,urq->cr", hidden, act_gradient, preferred_element_type=jnp.float32
        )
        through = jnp.einsum(
            "cr,urq->ucq", down_whole[layer_index], act_gradient, preferred_element_type=jnp.float32
        )
        upstream = (upstream.astype(jnp.float32) + through).astype(jnp.bfloat16)
        down_part, up_part = (
            lax.psum_scatter(
                down_part.astype(jnp.bfloat16), "chan", scatter_dimension=0, tiled=True
            ).astype(jnp.float32),
            lax.psum_scatter(
                up_part.astype(jnp.bfloat16), "chan", scatter_dimension=0, tiled=True
            ).astype(jnp.float32),
        )
        core_part = lax.psum_scatter(
            core_part.astype(jnp.bfloat16), "chan", scatter_dimension=1, tiled=True
        ).astype(jnp.float32)
        down_list[layer_index], core_list[layer_index], up_list[layer_index] = settle(
            down_part, core_part, up_part
        )
    upstream = lax.all_to_all(upstream, "chan", split_axis=1, concat_axis=0, tiled=True)
    return (upstream, down_list, core_list, up_list)


def local(
    features,
    cotangent,
    down_factor,
    core_kernel,
    up_factor,
    tile_count,
    neighbour_owner,
    neighbour_slot,
):
    upstream, down_list, core_list, up_list = whole_tiles(
        features,
        cotangent,
        down_factor,
        core_kernel,
        up_factor,
        tile_count,
        neighbour_owner,
        neighbour_slot,
    )
    down_gradient = jnp.stack(down_list, axis=0)
    core_gradient = jnp.stack(core_list, axis=0)
    up_gradient = jnp.stack(up_list, axis=0)
    down_gradient, core_gradient, up_gradient = lax.psum(
        (down_gradient, core_gradient, up_gradient), ("tiles", "sub")
    )
    return (upstream, down_gradient, core_gradient, up_gradient)


def solution(mesh):
    return jax.shard_map(
        local,
        mesh=mesh,
        in_specs=(
            P(("groups", "tiles", "sub"), "chan", None),
            P(("groups", "tiles", "sub"), "chan", None),
            P(None, "chan", None),
            P(),
            P(None, "chan", None),
            P(("groups", "tiles", "sub")),
            P(("groups", "tiles", "sub"), None),
            P(("groups", "tiles", "sub"), None),
        ),
        out_specs=(
            P(("groups", "tiles", "sub"), "chan", None),
            P("groups", "chan", None),
            P("groups", None, "chan", None),
            P("groups", "chan", None),
        ),
        check_vma=False,
    )
```

profile of v0, /device:TPU:0, one launch (start us, length us, event | category | flops | bytes accessed | tf_op | source)
XLA Modules:
  0.0 318.6 jit_solution(4942004799345471863)
XLA Ops:
  7.2 4.3 %all-to-all-start.1 = ((bf16[8,128,256]{2,1,0:T(8,128)(2,1)}), bf16[8,128,256]{2,1,0:T(8,128)(2,1)S(1)}, u32[]{:S(2)}, u32[]{:S(2)}) async-start(bf16[8,128,256]{2,1,0:T(8,128)(2,1)} %param.8), calls=%async_computation.1 | async-start | bytes 1048576 | tf_op jit(solution)/shard_map/all_to_all | solution.py:151
  13.7 6.6 %all-to-all-done.1 = bf16[8,128,256]{2,1,0:T(8,128)(2,1)S(1)} async-done(((bf16[8,128,256]{2,1,0:T(8,128)(2,1)}), bf16[8,128,256]{2,1,0:T(8,128)(2,1)S(1)}, u32[]{:S(2)}, u32[]{:S(2)}) %all-to-all-start.1) | async-done | bytes 524320 | tf_op jit(solution)/shard_map/all_to_all | solution.py:151
  20.3 3.5 %all-to-all-start = ((bf16[8,128,256]{2,1,0:T(8,128)(2,1)}), bf16[8,128,256]{2,1,0:T(8,128)(2,1)S(1)}, u32[]{:S(2)}, u32[]{:S(2)}) async-start(bf16[8,128,256]{2,1,0:T(8,128)(2,1)} %param.9), calls=%async_computation | async-start | bytes 1048576 | tf_op jit(solution)/shard_map/all_to_all | solution.py:152
  23.8 8.3 %all_gather.18 = bf16[2,256,64]{1,2,0:T(8,128)(2,1)S(1)} all-gather(bf16[2,128,64]{1,2,0:T(8,128)(2,1)S(1)} %copy-done.36), channel_id=1, replica_groups=mesh['groups'=2,'tiles'=4,'chan'=2,'sub'=2] {'chan'}, dimensions={1}, use_global_device_ids=true | all-gather | bytes 98304 | tf_op jit(solution)/shard_map/all_gather | solution.py:158
  32.2 4.6 %all_gather.20 = bf16[2,256,64]{1,2,0:T(8,128)(2,1)S(1)} all-gather(bf16[2,128,64]{1,2,0:T(8,128)(2,1)S(1)} %copy-done.37), channel_id=1, replica_groups=mesh['groups'=2,'tiles'=4,'chan'=2,'sub'=2] {'chan'}, dimensions={1}, use_global_device_ids=true | all-gather | bytes 98304 | tf_op jit(solution)/shard_map/all_gather | solution.py:159
  38.7 4.9 %all_gather.19 = bf16[8,64,68]{2,1,0:T(8,128)(2,1)S(1)} all-gather(bf16[4,64,68]{2,1,0:T(8,128)(2,1)S(1)} %copy.660), channel_id=1, replica_groups=mesh['groups'=2,'tiles'=4,'chan'=2,'sub'=2] {'chan'}, dimensions={0}, use_global_device_ids=true | all-gather | bytes 104448 | tf_op jit(solution)/shard_map/all_gather | solution.py:167
  43.8 1.3 collective-permute-start.1
  45.1 3.0 collective-permute-start
  54.6 1.4 add_convert_fusion
  57.4 4.9 %all_gather.21 = bf16[8,64,68]{2,1,0:T(8,128)(2,1)S(1)} all-gather(bf16[4,64,68]{2,1,0:T(8,128)(2,1)S(1)} %copy.692), channel_id=1, replica_groups=mesh['groups'=2,'tiles'=4,'chan'=2,'sub'=2] {'chan'}, dimensions={0}, use_global_device_ids=true | all-gather | bytes 104448 | tf_op jit(solution)/shard_map/all_gather | solution.py:167
  62.5 1.3 collective-permute-start.3
  63.8 3.5 %collective-permute-start.2 = (bf16[8,64,68]{1,0,2:T(8,128)(2,1)S(1)}, bf16[8,64,68]{1,0,2:T(8,128)(2,1)S(1)}, u32[]{:S(2)}, u32[]{:S(2)}) collective-permute-start(bf16[8,64,68]{1,0,2:T(8,128)(2,1)S(1)} %copy.693), channel_id=1, source_target_pairs={{0,1},{1,4},{4,5},{5,8},{8,9},{9,12},{12,13},{2,3},{3,6},{6,7},{7,... | collective-permute-start | bytes 208904 | tf_op jit(solution)/shard_map/ppermute | solution.py:22
  72.8 1.7 copy.716
  77.0 1.7 copy.711
  89.4 1.5 concatenate.146
  91.6 5.1 %all_gather.22 = bf16[8,64,68]{2,1,0:T(8,128)(2,1)S(1)} all-gather(bf16[4,64,68]{2,1,0:T(8,128)(2,1)} %copy.724), channel_id=1, replica_groups=mesh['groups'=2,'tiles'=4,'chan'=2,'sub'=2] {'chan'}, dimensions={0}, use_global_device_ids=true | all-gather | bytes 104448 | tf_op jit(solution)/shard_map/all_gather | solution.py:167
  97.5 6.0 %collective-permute-start.4 = (bf16[8,64,68]{2,0,1:T(8,128)(2,1)}, bf16[8,64,68]{2,0,1:T(8,128)(2,1)}, u32[]{:S(2)}, u32[]{:S(2)}) collective-permute-start(bf16[8,64,68]{2,0,1:T(8,128)(2,1)} %copy.725), channel_id=1, source_target_pairs={{0,1},{1,4},{4,5},{5,8},{8,9},{9,12},{12,13},{2,3},{3,6},{6,7},{7,... | collective-permute-start | bytes 208904 | tf_op jit(solution)/shard_map/ppermute | solution.py:22
  103.5 1.9 fusion.27
  105.5 1.3 collective-permute-start.5
  106.7 1.5 copy.811
  109.4 2.2 collective-permute-done.5
  112.8 1.9 copy.732
  116.2 1.4 fusion.76
  117.6 1.6 copy.738
  119.2 1.6 copy.733
  120.7 1.0 copy.729
  122.4 1.0 copy.728
  123.4 1.7 pad_maximum_fusion.10
  125.2 1.7 copy.745
  129.2 1.5 maximum_maximum_fusion.2
  131.7 1.7 copy.748
  133.4 1.7 copy.747
  135.1 1.7 copy.746
  137.9 1.8 copy.743
  139.6 1.7 copy.742
  141.4 1.8 copy.741
  147.4 1.3 fusion.31
  151.7 1.5 concatenate.155
  154.0 5.1 %all_gather.23 = bf16[8,64,68]{2,1,0:T(8,128)(2,1)S(1)} all-gather(bf16[4,64,68]{2,1,0:T(8,128)(2,1)} %copy.757), channel_id=1, replica_groups=mesh['groups'=2,'tiles'=4,'chan'=2,'sub'=2] {'chan'}, dimensions={0}, use_global_device_ids=true | all-gather | bytes 104448 | tf_op jit(solution)/shard_map/all_gather | solution.py:167
  159.8 4.9 %collective-permute-start.6 = (bf16[8,64,68]{2,0,1:T(8,128)(2,1)}, bf16[8,64,68]{2,0,1:T(8,128)(2,1)}, u32[]{:S(2)}, u32[]{:S(2)}) collective-permute-start(bf16[8,64,68]{2,0,1:T(8,128)(2,1)} %copy.758), channel_id=1, source_target_pairs={{0,1},{1,4},{4,5},{5,8},{8,9},{9,12},{12,13},{2,3},{3,6},{6,7},{7,... | collective-permute-start | bytes 208904 | tf_op jit(solution)/shard_map/ppermute | solution.py:22
  164.9 2.0 fusion.25
  166.8 1.3 collective-permute-start.7
  168.1 1.5 copy.807
  172.8 1.9 copy.765
  176.2 1.4 fusion.74
  177.6 1.6 copy.771
  180.2 1.0 copy.762
  181.9 1.0 copy.761
  182.9 1.7 pad_maximum_fusion.8
  184.7 1.7 copy.778
  188.6 1.5 maximum_maximum_fusion.3
  191.1 1.7 copy.781
  192.9 1.7 copy.780
  194.6 1.7 copy.779
  197.3 1.8 copy.776
  199.1 1.7 copy.775
  200.8 1.8 copy.774
  213.6 1.2 copy.784
  214.8 3.5 %all-to-all-start.2 = ((bf16[4,256,256]{2,0,1:T(4,128)(2,1)}), bf16[4,256,256]{2,0,1:T(4,128)(2,1)S(1)}, u32[]{:S(2)}, u32[]{:S(2)}) async-start(bf16[4,256,256]{2,0,1:T(4,128)(2,1)} %copy.784), calls=%async_computation.2 | async-start | bytes 1048576 | tf_op jit(solution)/shard_map/all_to_all | solution.py:216
  220.6 12.8 %reduce-scatter.17.cloned.1.call-done = bf16[9,32,64]{2,0,1:T(8,128)(2,1)} async-done(((bf16[9,64,64]{2,0,1:T(8,128)(2,1)}), bf16[9,32,64]{2,0,1:T(8,128)(2,1)}) %reduce-scatter.17.cloned.1.call-update) | async-done | bytes 36880 | tf_op jit(solution)/shard_map/reduce_scatter | solution.py:210
  233.5 13.9 %reduce-scatter.15.cloned.1.call-done = bf16[9,32,64]{2,0,1:T(8,128)(2,1)} async-done(((bf16[9,64,64]{2,0,1:T(8,128)(2,1)}), bf16[9,32,64]{2,0,1:T(8,128)(2,1)}) %reduce-scatter.15.cloned.1.call-update) | async-done | bytes 36880 | tf_op jit(solution)/shard_map/reduce_scatter | solution.py:210
  247.4 1.9 maximum_convert_fusion
  249.2 58.5 %all-reduce.3.cloned.1.call-done = (f32[2,128,64]{1,2,0:T(8,128)}, f32[2,9,32,64]{3,1,2,0:T(8,128)}, f32[2,128,64]{1,2,0:T(8,128)}) async-done(((f32[2,128,64]{1,2,0:T(8,128)}, f32[2,9,32,64]{3,1,2,0:T(8,128)}, f32[2,128,64]{1,2,0:T(8,128)}), (f32[2,128,64]{1,2,0:T(8,128)}, f32[2,9,32,64]{3,1,2,0:T(8,128)}, f32[2,128,64]{1,2,0:T(8,128)})) %all-reduce.3.cloned.1.call-update) | async-done | bytes 278544 | tf_op jit(solution)/shard_map/psum | solution.py:243
  307.7 1.9 copy.788
  (298 shorter events, 74.1 us)
Async XLA Ops:
  7.2 16.7 %copy-start.36 = (bf16[2,128,64]{1,2,0:T(8,128)(2,1)S(1)}, bf16[2,128,64]{1,2,0:T(8,128)(2,1)}, u32[]{:S(2)}) copy-start(bf16[2,128,64]{1,2,0:T(8,128)(2,1)} %param.10) | copy-start | bytes 98308
  7.2 25.0 %copy-start.37 = (bf16[2,128,64]{1,2,0:T(8,128)(2,1)S(1)}, bf16[2,128,64]{1,2,0:T(8,128)(2,1)}, u32[]{:S(2)}) copy-start(bf16[2,128,64]{1,2,0:T(8,128)(2,1)} %param.12) | copy-start | bytes 98308
  7.2 13.1 %all-to-all-start.1 = ((bf16[8,128,256]{2,1,0:T(8,128)(2,1)}), bf16[8,128,256]{2,1,0:T(8,128)(2,1)S(1)}, u32[]{:S(2)}, u32[]{:S(2)}) async-start(bf16[8,128,256]{2,1,0:T(8,128)(2,1)} %param.8), calls=%async_computation.1 | async-start | bytes 1048576 | tf_op jit(solution)/shard_map/all_to_all | solution.py:151
  20.3 16.6 %all-to-all-start = ((bf16[8,128,256]{2,1,0:T(8,128)(2,1)}), bf16[8,128,256]{2,1,0:T(8,128)(2,1)S(1)}, u32[]{:S(2)}, u32[]{:S(2)}) async-start(bf16[8,128,256]{2,1,0:T(8,128)(2,1)} %param.9), calls=%async_computation | async-start | bytes 1048576 | tf_op jit(solution)/shard_map/all_to_all | solution.py:152
  23.8 184.8 %reduce-scatter.25.cloned.1.call-start = ((), (), s32[]{:S(2)}) async-start(), calls=%async_computation.14 | async-start | bytes 98304
  32.2 24.1 %copy-start.26 = (bf16[2,256,64]{1,2,0:T(8,128)(2,1)}, bf16[2,256,64]{1,2,0:T(8,128)(2,1)S(1)}, u32[]{:S(2)}) copy-start(bf16[2,256,64]{1,2,0:T(8,128)(2,1)S(1)} %all_gather.18) | copy-start | bytes 196612
  36.8 17.9 %copy-start.31 = (bf16[2,256,64]{1,2,0:T(8,128)(2,1)}, bf16[2,256,64]{1,2,0:T(8,128)(2,1)S(1)}, u32[]{:S(2)}) copy-start(bf16[2,256,64]{1,2,0:T(8,128)(2,1)S(1)} %all_gather.20) | copy-start | bytes 196612
  43.8 4.4 %collective-permute-start.1 = (bf16[8,64,68]{1,0,2:T(8,128)(2,1)S(1)}, bf16[8,64,68]{1,0,2:T(8,128)(2,1)S(1)}, u32[]{:S(2)}, u32[]{:S(2)}) collective-permute-start(bf16[8,64,68]{1,0,2:T(8,128)(2,1)S(1)} %copy.661), channel_id=1, source_target_pairs={{1,0},{4,1},{5,4},{8,5},{9,8},{12,9},{13,12},{3,2},{6,3},{7,6},{10... | collective-permute-start | bytes 208904 | tf_op jit(solution)/shard_map/ppermute | solution.py:24
  45.1 4.0 %collective-permute-start = (bf16[8,64,68]{1,0,2:T(8,128)(2,1)S(1)}, bf16[8,64,68]{1,0,2:T(8,128)(2,1)S(1)}, u32[]{:S(2)}, u32[]{:S(2)}) collective-permute-start(bf16[8,64,68]{1,0,2:T(8,128)(2,1)S(1)} %copy.661), channel_id=1, source_target_pairs={{0,1},{1,4},{4,5},{5,8},{8,9},{9,12},{12,13},{2,3},{3,6},{6,7},{7,... | collective-permute-start | bytes 208904 | tf_op jit(solution)/shard_map/ppermute | solution.py:22
  53.3 1.0 copy-start.6
  54.6 1.4 copy-start.23
  56.1 0.8 copy-start.4
  62.5 4.8 %collective-permute-start.3 = (bf16[8,64,68]{1,0,2:T(8,128)(2,1)S(1)}, bf16[8,64,68]{1,0,2:T(8,128)(2,1)S(1)}, u32[]{:S(2)}, u32[]{:S(2)}) collective-permute-start(bf16[8,64,68]{1,0,2:T(8,128)(2,1)S(1)} %copy.693), channel_id=1, source_target_pairs={{1,0},{4,1},{5,4},{8,5},{9,8},{12,9},{13,12},{3,2},{6,3},{7,6},{10... | collective-permute-start | bytes 208904 | tf_op jit(solution)/shard_map/ppermute | solution.py:24
  63.8 4.5 %collective-permute-start.2 = (bf16[8,64,68]{1,0,2:T(8,128)(2,1)S(1)}, bf16[8,64,68]{1,0,2:T(8,128)(2,1)S(1)}, u32[]{:S(2)}, u32[]{:S(2)}) collective-permute-start(bf16[8,64,68]{1,0,2:T(8,128)(2,1)S(1)} %copy.693), channel_id=1, source_target_pairs={{0,1},{1,4},{4,5},{5,8},{8,9},{9,12},{12,13},{2,3},{3,6},{6,7},{7,... | collective-permute-start | bytes 208904 | tf_op jit(solution)/shard_map/ppermute | solution.py:22
  80.3 5.7 %copy-start.16 = (bf16[1,4,64,256]{3,2,1,0:T(8,128)(2,1)S(1)}, bf16[1,4,64,256]{3,2,1,0:T(8,128)(2,1)}, u32[]{:S(2)}) copy-start(bf16[1,4,64,256]{3,2,1,0:T(8,128)(2,1)} %copy.716) | copy-start | bytes 393220
  84.0 2.3 copy-start.9
  84.0 2.3 copy-start.32
  87.0 0.8 copy-start.5
  88.0 35.4 %copy-start.1 = (bf16[4,64,256]{1,2,0:T(8,128)(2,1)}, bf16[4,64,256]{1,2,0:T(8,128)(2,1)S(1)}, u32[]{:S(2)}) copy-start(bf16[4,64,256]{1,2,0:T(8,128)(2,1)S(1)} %copy.718) | copy-start | bytes 393220
  97.5 10.8 %collective-permute-start.4 = (bf16[8,64,68]{2,0,1:T(8,128)(2,1)}, bf16[8,64,68]{2,0,1:T(8,128)(2,1)}, u32[]{:S(2)}, u32[]{:S(2)}) collective-permute-start(bf16[8,64,68]{2,0,1:T(8,128)(2,1)} %copy.725), channel_id=1, source_target_pairs={{0,1},{1,4},{4,5},{5,8},{8,9},{9,12},{12,13},{2,3},{3,6},{6,7},{7,... | collective-permute-start | bytes 208904 | tf_op jit(solution)/shard_map/ppermute | solution.py:22
  105.5 6.1 %collective-permute-start.5 = (bf16[8,64,68]{2,0,1:T(8,128)(2,1)}, bf16[8,64,68]{2,0,1:T(8,128)(2,1)S(1)}, u32[]{:S(2)}, u32[]{:S(2)}) collective-permute-start(bf16[8,64,68]{2,0,1:T(8,128)(2,1)} %copy.725), channel_id=1, source_target_pairs={{1,0},{4,1},{5,4},{8,5},{9,8},{12,9},{13,12},{3,2},{6,3},{7,6},{10... | collective-permute-start | bytes 208904 | tf_op jit(solution)/shard_map/ppermute | solution.py:24
  108.3 102.6 %reduce-scatter.23.cloned.1.call-start = ((), (), s32[]{:S(2)}) async-start(), calls=%async_computation.13 | async-start | bytes 98304
  123.4 1.8 copy-start.29
  137.8 8.1 %copy-start.14 = (bf16[1,4,64,256]{3,2,1,0:T(8,128)(2,1)S(1)}, bf16[1,4,64,256]{3,2,1,0:T(8,128)(2,1)}, u32[]{:S(2)}) copy-start(bf16[1,4,64,256]{3,2,1,0:T(8,128)(2,1)} %copy.744) | copy-start | bytes 393220
  137.8 8.1 %copy-start.12 = (bf16[1,4,64,256]{3,2,1,0:T(8,128)(2,1)S(1)}, bf16[1,4,64,256]{3,2,1,0:T(8,128)(2,1)}, u32[]{:S(2)}) copy-start(bf16[1,4,64,256]{3,2,1,0:T(8,128)(2,1)} %copy.745) | copy-start | bytes 393220
  141.4 4.7 %copy-start.19 = (bf16[1,4,64,256]{3,2,1,0:T(8,128)(2,1)S(1)}, bf16[1,4,64,256]{3,2,1,0:T(8,128)(2,1)}, u32[]{:S(2)}) copy-start(bf16[1,4,64,256]{3,2,1,0:T(8,128)(2,1)} %copy.747) | copy-start | bytes 393220
  141.4 4.8 %copy-start.17 = (bf16[1,4,64,256]{3,2,1,0:T(8,128)(2,1)S(1)}, bf16[1,4,64,256]{3,2,1,0:T(8,128)(2,1)}, u32[]{:S(2)}) copy-start(bf16[1,4,64,256]{3,2,1,0:T(8,128)(2,1)} %copy.748) | copy-start | bytes 393220
  143.1 2.9 copy-start.21
  143.1 3.0 copy-start.7
  146.0 1.0 copy-start.10
  146.0 1.0 copy-start.27
  146.0 1.4 copy-start.38
  146.5 2.3 copy-start.25
  147.4 1.4 copy-start.24
  147.4 1.6 copy-start.33
  149.5 20.1 %copy-start.2 = (bf16[4,64,256]{2,1,0:T(8,128)(2,1)}, bf16[4,64,256]{2,1,0:T(8,128)(2,1)S(1)}, u32[]{:S(2)}) copy-start(bf16[4,64,256]{2,1,0:T(8,128)(2,1)S(1)} %add_convert_fusion.1) | copy-start | bytes 393220
  149.7 33.2 %copy-start = (bf16[4,64,256]{1,2,0:T(8,128)(2,1)}, bf16[4,64,256]{1,2,0:T(8,128)(2,1)S(1)}, u32[]{:S(2)}) copy-start(bf16[4,64,256]{1,2,0:T(8,128)(2,1)S(1)} %copy.751) | copy-start | bytes 393220
  159.8 9.8 %collective-permute-start.6 = (bf16[8,64,68]{2,0,1:T(8,128)(2,1)}, bf16[8,64,68]{2,0,1:T(8,128)(2,1)}, u32[]{:S(2)}, u32[]{:S(2)}) collective-permute-start(bf16[8,64,68]{2,0,1:T(8,128)(2,1)} %copy.758), channel_id=1, source_target_pairs={{0,1},{1,4},{4,5},{5,8},{8,9},{9,12},{12,13},{2,3},{3,6},{6,7},{7,... | collective-permute-start | bytes 208904 | tf_op jit(solution)/shard_map/ppermute | solution.py:22
  164.8 47.6 %reduce-scatter.21.cloned.1.call-start = ((), (), s32[]{:S(2)}) async-start(), calls=%async_computation.12 | async-start | bytes 98304
  166.8 3.9 %collective-permute-start.7 = (bf16[8,64,68]{2,0,1:T(8,128)(2,1)}, bf16[8,64,68]{2,0,1:T(8,128)(2,1)}, u32[]{:S(2)}, u32[]{:S(2)}) collective-permute-start(bf16[8,64,68]{2,0,1:T(8,128)(2,1)} %copy.758), channel_id=1, source_target_pairs={{1,0},{4,1},{5,4},{8,5},{9,8},{12,9},{13,12},{3,2},{6,3},{7,6},{10... | collective-permute-start | bytes 208904 | tf_op jit(solution)/shard_map/ppermute | solution.py:24
  169.6 49.5 %reduce-scatter.19.cloned.1.call-start = ((), (), s32[]{:S(2)}) async-start(), calls=%async_computation.11 | async-start | bytes 98304
  182.9 1.7 copy-start.30
  197.3 8.1 %copy-start.15 = (bf16[1,4,64,256]{3,2,1,0:T(8,128)(2,1)S(1)}, bf16[1,4,64,256]{3,2,1,0:T(8,128)(2,1)}, u32[]{:S(2)}) copy-start(bf16[1,4,64,256]{3,2,1,0:T(8,128)(2,1)} %copy.777) | copy-start | bytes 393220
  197.3 8.1 %copy-start.3 = (bf16[4,64,256]{2,1,0:T(8,128)(2,1)S(1)}, bf16[4,64,256]{2,1,0:T(8,128)(2,1)}, u32[]{:S(2)}) copy-start(bf16[4,64,256]{2,1,0:T(8,128)(2,1)} %copy-done.2) | copy-start | bytes 393220
  197.3 8.2 %copy-start.13 = (bf16[1,4,64,256]{3,2,1,0:T(8,128)(2,1)S(1)}, bf16[1,4,64,256]{3,2,1,0:T(8,128)(2,1)}, u32[]{:S(2)}) copy-start(bf16[1,4,64,256]{3,2,1,0:T(8,128)(2,1)} %copy.778) | copy-start | bytes 393220
  200.8 4.7 %copy-start.18 = (bf16[1,4,64,256]{3,2,1,0:T(8,128)(2,1)S(1)}, bf16[1,4,64,256]{3,2,1,0:T(8,128)(2,1)}, u32[]{:S(2)}) copy-start(bf16[1,4,64,256]{3,2,1,0:T(8,128)(2,1)} %copy.781) | copy-start | bytes 393220
  202.6 2.9 copy-start.22
  202.6 2.9 copy-start.20
  202.6 3.0 copy-start.8
  207.0 26.5 %reduce-scatter.17.cloned.1.call-start = ((), (), s32[]{:S(2)}) async-start(), calls=%async_computation.10 | async-start | bytes 393216 | tf_op jit(solution)/shard_map/reduce_scatter | solution.py:210
  208.5 38.9 %reduce-scatter.15.cloned.1.call-start = ((), (), s32[]{:S(2)}) async-start(), calls=%async_computation.9 | async-start | bytes 393216 | tf_op jit(solution)/shard_map/reduce_scatter | solution.py:210
  209.4 3.8 %copy-start.11 = (bf16[4,256,256]{2,1,0:T(8,128)(2,1)S(1)}, bf16[4,256,256]{2,1,0:T(8,128)(2,1)}, u32[]{:S(2)}) copy-start(bf16[4,256,256]{2,1,0:T(8,128)(2,1)} %get-tuple-element.146) | copy-start | bytes 1572868
  209.4 3.8 %copy-start.28 = (bf16[2,256,64]{1,2,0:T(8,128)(2,1)S(1)}, bf16[2,256,64]{1,2,0:T(8,128)(2,1)}, u32[]{:S(2)}) copy-start(bf16[2,256,64]{1,2,0:T(8,128)(2,1)} %copy-done.26) | copy-start | bytes 196612
  214.8 94.8 %all-to-all-start.2 = ((bf16[4,256,256]{2,0,1:T(4,128)(2,1)}), bf16[4,256,256]{2,0,1:T(4,128)(2,1)S(1)}, u32[]{:S(2)}, u32[]{:S(2)}) async-start(bf16[4,256,256]{2,0,1:T(4,128)(2,1)} %copy.784), calls=%async_computation.2 | async-start | bytes 1048576 | tf_op jit(solution)/shard_map/all_to_all | solution.py:216
  218.3 89.4 %all-reduce.3.cloned.1.call-start = ((), (), s32[]{:S(2)}) async-start(), calls=%async_computation.15 | async-start | bytes 1310720 | tf_op jit(solution)/shard_map/psum | solution.py:243
  307.7 2.8 copy-start.35
  307.7 3.4 %copy-start.34 = (f32[2,128,64]{1,2,0:T(8,128)S(1)}, f32[2,128,64]{1,2,0:T(8,128)}, u32[]{:S(2)}) copy-start(f32[2,128,64]{1,2,0:T(8,128)} %get-tuple-element.152) | copy-start | bytes 196612
Sparse Core Ops, SparseCore 0:
  108.4 13.9 reduce-scatter.24
  164.9 9.3 reduce-scatter.22
  177.1 9.8 reduce-scatter.20
  207.1 11.9 reduce-scatter.18
  221.8 11.6 reduce-scatter.16
  235.6 11.6 reduce-scatter.14
  250.5 57.1 all-reduce.2
where the time goes:
time: 321 us; the launch traced here: 319 us
  local copies, waits for them, and re-layouts  106 us (33%)
  waiting for transfers between devices  96.8 us (30%)
  starting transfers between devices  34.3 us (11%)
  blocking collectives  33.1 us (10%)
  other arithmetic  16.8 us (5%)
  between operations  16.2 us (5%)
  matrix products  15 us (5%)
    psum x1, waiting for transfers between devices, local(): lax.psum((down_gradient, core_gradient, up_gradient), ('tiles', 'sub'))  58.5 us
    unnamed x132, local copies, waits for them, and re-layouts  27.1 us
    reduce_scatter x2, waiting for transfers between devices, whole_tiles(): lax.psum_scatter(core_part.astype(jnp.bfloat16), 'chan', scatter_dimensio...  26.7 us
    another operation x18, local copies, waits for them, and re-layouts, stacked_windows(): jnp.stack([window(padded, 2 - offset // 3, 2 - offset % 3) for offset in...  25.9 us
    all_gather x4, blocking collectives, padded_of(): owner_cycle = lax.all_gather(border, 'chan', axis=0, tiled=True)  20.2 us
    ppermute x4, starting transfers between devices, padded_2(): lax.ppermute(tail, axis, [(i, (i + 1) % count) for i in range(ends)])  17.6 us
    slice x20, local copies, waits for them, and re-layouts, place_border(): nearest[:, which_side, :, piece_index * TILE:(piece_index + 1) * TILE]  14.6 us
    another operation x18, local copies, waits for them, and re-layouts, stacked_windows(): jnp.stack([window(padded, offset // 3, offset % 3) for offset in range(9)...  8.53 us
  transfers between devices with their start and end apart: 18, of which 8 were waited for; matrix products, arithmetic and copies ran while one was open for 32% of the time, Pallas kernels for 0%

commit v1 on v0

--- a/solution.py
+++ b/solution.py
@@ -1,3 +1,4 @@
+import functools
 import jax
 import jax.numpy as jnp
 from jax import lax
@@ -9,6 +10,14 @@
 EDGE_PIECES = [1, 0, 3, 2]
 CORNER_ROWS = [0, 2, 5, 7]
 CORNER_PIECES = [3, 2, 1, 0]
+
+
+def vectors_tell(message, across, axis_key):
+    spare = jax.lax.psum(jax.lax.psum(message, across), axis_name=axis_key)
+    return spare
+
+
+remake_the_ends = functools.partial(vectors_tell, across="sub", axis_key="tiles")
 
 
 def padded_2(cells, sides, width):
@@ -240,8 +249,8 @@
     down_gradient = jnp.stack(down_list, axis=0)
     core_gradient = jnp.stack(core_list, axis=0)
     up_gradient = jnp.stack(up_list, axis=0)
-    down_gradient, core_gradient, up_gradient = lax.psum(
-        (down_gradient, core_gradient, up_gradient), ("tiles", "sub")
+    down_gradient, core_gradient, up_gradient = remake_the_ends(
+        (down_gradient, core_gradient, up_gradient)
     )
     return (upstream, down_gradient, core_gradient, up_gradient)
 

time: 321 us -> 329 us (1.025)
  blocking collectives: 33.1 us -> 44.3 us
  starting transfers between devices: 34.3 us -> 30.9 us
    all_to_all x0 -> x1, blocking collectives: none -> 11.2 us  [whole_tiles(): lax.all_to_all(upstream, 'chan', split_axis=1, concat_axis=0, tiled=True)]
    psum x1 -> x2, waiting for transfers between devices: 58.5 us -> 52.4 us  [vectors_tell(): spare = jax.lax.psum(jax.lax.psum(message, across), axis_name=axis_key)]
    unnamed x11 -> x12, waiting for transfers between devices: 0.97 us -> 6.01 us
    all_to_all x1 -> x0, starting transfers between devices: 3.49 us -> none  [whole_tiles(): lax.all_to_all(upstream, 'chan', split_axis=1, concat_axis=0, tiled=True)]
    unnamed x132 -> x128, local copies, waits for them, and re-layouts: 27.1 us -> 28.8 us
  transfers between devices with their start and end apart: 18 -> 18, of which waited for: 8 -> 9; matrix products, arithmetic and copies ran while one was open for 32% -> 30% of each run, Pallas kernels for 0% -> 0%
where the time goes in v1:
time: 329 us; the launch traced here: 326 us
  local copies, waits for them, and re-layouts  107 us (33%)
  waiting for transfers between devices  95.8 us (29%)
  blocking collectives  44.3 us (13%)
  starting transfers between devices  30.9 us (9%)
  other arithmetic  16.8 us (5%)
  between operations  16.2 us (5%)
  matrix products  15 us (5%)
    psum x2, waiting for transfers between devices, vectors_tell(): spare = jax.lax.psum(jax.lax.psum(message, across), axis_name=axis_key)  52.4 us
    unnamed x128, local copies, waits for them, and re-layouts  28.8 us
    reduce_scatter x2, waiting for transfers between devices, whole_tiles(): lax.psum_scatter(core_part.astype(jnp.bfloat16), 'chan', scatter_dimensio...  26.7 us
    another operation x18, local copies, waits for them, and re-layouts, stacked_windows(): jnp.stack([window(padded, 2 - offset // 3, 2 - offset % 3) for offset in...  25.9 us
    all_gather x4, blocking collectives, padded_of(): owner_cycle = lax.all_gather(border, 'chan', axis=0, tiled=True)  20.2 us
    ppermute x4, starting transfers between devices, padded_2(): lax.ppermute(tail, axis, [(i, (i + 1) % count) for i in range(ends)])  17.6 us
    slice x20, local copies, waits for them, and re-layouts, place_border(): nearest[:, which_side, :, piece_index * TILE:(piece_index + 1) * TILE]  14.6 us
    all_to_all x1, blocking collectives, whole_tiles(): lax.all_to_all(upstream, 'chan', split_axis=1, concat_axis=0, tiled=True)  11.2 us
  transfers between devices with their start and end apart: 18, of which 9 were waited for; matrix products, arithmetic and copies ran while one was open for 30% of the time, Pallas kernels for 0%

profile of v1, /device:TPU:0, one launch (start us, length us, event | category | flops | bytes accessed | tf_op | source)
XLA Modules:
  0.0 326.3 jit_solution(10704132441250115852)
XLA Ops:
  7.2 4.3 %all-to-all-start.1 = ((bf16[8,128,256]{2,1,0:T(8,128)(2,1)}), bf16[8,128,256]{2,1,0:T(8,128)(2,1)S(1)}, u32[]{:S(2)}, u32[]{:S(2)}) async-start(bf16[8,128,256]{2,1,0:T(8,128)(2,1)} %param.8), calls=%async_computation.1 | async-start | bytes 1048576 | tf_op jit(solution)/shard_map/all_to_all | solution.py:160
  13.7 6.6 %all-to-all-done.1 = bf16[8,128,256]{2,1,0:T(8,128)(2,1)S(1)} async-done(((bf16[8,128,256]{2,1,0:T(8,128)(2,1)}), bf16[8,128,256]{2,1,0:T(8,128)(2,1)S(1)}, u32[]{:S(2)}, u32[]{:S(2)}) %all-to-all-start.1) | async-done | bytes 524320 | tf_op jit(solution)/shard_map/all_to_all | solution.py:160
  20.3 3.5 %all-to-all-start = ((bf16[8,128,256]{2,1,0:T(8,128)(2,1)}), bf16[8,128,256]{2,1,0:T(8,128)(2,1)S(1)}, u32[]{:S(2)}, u32[]{:S(2)}) async-start(bf16[8,128,256]{2,1,0:T(8,128)(2,1)} %param.9), calls=%async_computation | async-start | bytes 1048576 | tf_op jit(solution)/shard_map/all_to_all | solution.py:161
  23.8 8.3 %all_gather.18 = bf16[2,256,64]{1,2,0:T(8,128)(2,1)S(1)} all-gather(bf16[2,128,64]{1,2,0:T(8,128)(2,1)S(1)} %copy-done.34), channel_id=1, replica_groups=mesh['groups'=2,'tiles'=4,'chan'=2,'sub'=2] {'chan'}, dimensions={1}, use_global_device_ids=true | all-gather | bytes 98304 | tf_op jit(solution)/shard_map/all_gather | solution.py:167
  32.2 4.6 %all_gather.20 = bf16[2,256,64]{1,2,0:T(8,128)(2,1)S(1)} all-gather(bf16[2,128,64]{1,2,0:T(8,128)(2,1)S(1)} %copy-done.35), channel_id=1, replica_groups=mesh['groups'=2,'tiles'=4,'chan'=2,'sub'=2] {'chan'}, dimensions={1}, use_global_device_ids=true | all-gather | bytes 98304 | tf_op jit(solution)/shard_map/all_gather | solution.py:168
  38.7 4.9 %all_gather.19 = bf16[8,64,68]{2,1,0:T(8,128)(2,1)S(1)} all-gather(bf16[4,64,68]{2,1,0:T(8,128)(2,1)S(1)} %copy.660), channel_id=1, replica_groups=mesh['groups'=2,'tiles'=4,'chan'=2,'sub'=2] {'chan'}, dimensions={0}, use_global_device_ids=true | all-gather | bytes 104448 | tf_op jit(solution)/shard_map/all_gather | solution.py:176
  43.8 1.3 collective-permute-start.1
  45.1 3.0 collective-permute-start
  54.6 1.4 add_convert_fusion
  57.4 4.9 %all_gather.21 = bf16[8,64,68]{2,1,0:T(8,128)(2,1)S(1)} all-gather(bf16[4,64,68]{2,1,0:T(8,128)(2,1)S(1)} %copy.692), channel_id=1, replica_groups=mesh['groups'=2,'tiles'=4,'chan'=2,'sub'=2] {'chan'}, dimensions={0}, use_global_device_ids=true | all-gather | bytes 104448 | tf_op jit(solution)/shard_map/all_gather | solution.py:176
  62.5 1.3 collective-permute-start.3
  63.8 3.5 %collective-permute-start.2 = (bf16[8,64,68]{1,0,2:T(8,128)(2,1)S(1)}, bf16[8,64,68]{1,0,2:T(8,128)(2,1)S(1)}, u32[]{:S(2)}, u32[]{:S(2)}) collective-permute-start(bf16[8,64,68]{1,0,2:T(8,128)(2,1)S(1)} %copy.693), channel_id=1, source_target_pairs={{0,1},{1,4},{4,5},{5,8},{8,9},{9,12},{12,13},{2,3},{3,6},{6,7},{7,... | collective-permute-start | bytes 208904 | tf_op jit(solution)/shard_map/ppermute | solution.py:31
  72.8 1.7 copy.716
  77.0 1.7 copy.711
  89.4 1.5 concatenate.146
  91.6 5.1 %all_gather.22 = bf16[8,64,68]{2,1,0:T(8,128)(2,1)S(1)} all-gather(bf16[4,64,68]{2,1,0:T(8,128)(2,1)} %copy.724), channel_id=1, replica_groups=mesh['groups'=2,'tiles'=4,'chan'=2,'sub'=2] {'chan'}, dimensions={0}, use_global_device_ids=true | all-gather | bytes 104448 | tf_op jit(solution)/shard_map/all_gather | solution.py:176
  97.5 6.0 %collective-permute-start.4 = (bf16[8,64,68]{2,0,1:T(8,128)(2,1)}, bf16[8,64,68]{2,0,1:T(8,128)(2,1)}, u32[]{:S(2)}, u32[]{:S(2)}) collective-permute-start(bf16[8,64,68]{2,0,1:T(8,128)(2,1)} %copy.725), channel_id=1, source_target_pairs={{0,1},{1,4},{4,5},{5,8},{8,9},{9,12},{12,13},{2,3},{3,6},{6,7},{7,... | collective-permute-start | bytes 208904 | tf_op jit(solution)/shard_map/ppermute | solution.py:31
  103.5 1.9 fusion.27
  105.5 1.3 collective-permute-start.5
  106.8 1.5 copy.811
  109.4 2.2 collective-permute-done.5
  112.8 1.9 copy.732
  116.1 1.4 fusion.76
  117.5 1.6 copy.738
  119.1 1.6 copy.733
  123.4 1.7 pad_maximum_fusion.10
  125.2 1.7 copy.745
  129.1 1.5 maximum_maximum_fusion.2
  131.7 1.7 copy.748
  133.4 1.7 copy.747
  135.1 1.7 copy.746
  137.8 1.8 copy.743
  139.6 1.7 copy.742
  141.3 1.8 copy.741
  147.4 1.3 fusion.31
  151.7 1.5 concatenate.155
  153.9 5.1 %all_gather.23 = bf16[8,64,68]{2,1,0:T(8,128)(2,1)S(1)} all-gather(bf16[4,64,68]{2,1,0:T(8,128)(2,1)} %copy.757), channel_id=1, replica_groups=mesh['groups'=2,'tiles'=4,'chan'=2,'sub'=2] {'chan'}, dimensions={0}, use_global_device_ids=true | all-gather | bytes 104448 | tf_op jit(solution)/shard_map/all_gather | solution.py:176
  159.8 4.9 %collective-permute-start.6 = (bf16[8,64,68]{2,0,1:T(8,128)(2,1)}, bf16[8,64,68]{2,0,1:T(8,128)(2,1)}, u32[]{:S(2)}, u32[]{:S(2)}) collective-permute-start(bf16[8,64,68]{2,0,1:T(8,128)(2,1)} %copy.758), channel_id=1, source_target_pairs={{0,1},{1,4},{4,5},{5,8},{8,9},{9,12},{12,13},{2,3},{3,6},{6,7},{7,... | collective-permute-start | bytes 208904 | tf_op jit(solution)/shard_map/ppermute | solution.py:31
  164.8 2.0 fusion.25
  166.8 1.3 collective-permute-start.7
  168.1 1.5 copy.807
  172.8 1.9 copy.765
  176.2 1.4 fusion.74
  177.6 1.6 copy.771
  180.2 1.0 copy.762
  182.9 1.7 pad_maximum_fusion.8
  184.7 1.7 copy.778
  188.6 1.5 maximum_maximum_fusion.3
  191.1 1.7 copy.781
  192.9 1.7 copy.780
  194.6 1.7 copy.779
  197.3 1.8 copy.776
  199.1 1.7 copy.775
  200.8 1.8 copy.774
  213.3 5.8 %reduce-scatter.19.cloned.1.call-done = bf16[128,64]{1,0:T(8,128)(2,1)} async-done(((bf16[256,64]{1,0:T(8,128)(2,1)}), bf16[128,64]{1,0:T(8,128)(2,1)}) %reduce-scatter.19.cloned.1.call-update) | async-done | bytes 16400
  220.7 12.8 %reduce-scatter.17.cloned.1.call-done = bf16[9,32,64]{2,0,1:T(8,128)(2,1)} async-done(((bf16[9,64,64]{2,0,1:T(8,128)(2,1)}), bf16[9,32,64]{2,0,1:T(8,128)(2,1)}) %reduce-scatter.17.cloned.1.call-update) | async-done | bytes 36880 | tf_op jit(solution)/shard_map/reduce_scatter | solution.py:219
  233.5 13.9 %reduce-scatter.15.cloned.1.call-done = bf16[9,32,64]{2,0,1:T(8,128)(2,1)} async-done(((bf16[9,64,64]{2,0,1:T(8,128)(2,1)}), bf16[9,32,64]{2,0,1:T(8,128)(2,1)}) %reduce-scatter.15.cloned.1.call-update) | async-done | bytes 36880 | tf_op jit(solution)/shard_map/reduce_scatter | solution.py:219
  247.4 1.8 maximum_convert_fusion
  249.3 20.3 %all-reduce.7.cloned.1.call-done = (f32[2,128,64]{1,2,0:T(8,128)}, f32[2,9,32,64]{3,1,2,0:T(8,128)}, f32[2,128,64]{1,2,0:T(8,128)}) async-done(((f32[2,128,64]{1,2,0:T(8,128)}, f32[2,9,32,64]{3,1,2,0:T(8,128)}, f32[2,128,64]{1,2,0:T(8,128)}), (f32[2,128,64]{1,2,0:T(8,128)}, f32[2,9,32,64]{3,1,2,0:T(8,128)}, f32[2,128,64]{1,2,0:T(8,128)})) %all-reduce.7.cloned.1.call-update) | async-done | bytes 278544 | tf_op jit(solution)/shard_map/psum | solution.py:16
  270.4 11.2 %all_to_all.54 = bf16[4,256,256]{2,0,1:T(4,128)(2,1)S(1)} all-to-all(bf16[4,256,256]{2,0,1:T(4,128)(2,1)S(1)} %copy.784), channel_id=1, replica_groups=mesh['groups'=2,'tiles'=4,'chan'=2,'sub'=2] {'chan'}, dimensions={1} | all-to-all | bytes 1048576 | tf_op jit(solution)/shard_map/all_to_all | solution.py:225
  282.5 32.2 %all-reduce.5.cloned.1.call-done = (f32[2,128,64]{1,2,0:T(8,128)}, f32[2,9,32,64]{3,1,2,0:T(8,128)}, f32[2,128,64]{1,2,0:T(8,128)}) async-done(((f32[2,128,64]{1,2,0:T(8,128)}, f32[2,9,32,64]{3,1,2,0:T(8,128)}, f32[2,128,64]{1,2,0:T(8,128)}), (f32[2,128,64]{1,2,0:T(8,128)}, f32[2,9,32,64]{3,1,2,0:T(8,128)}, f32[2,128,64]{1,2,0:T(8,128)})) %all-reduce.5.cloned.1.call-update) | async-done | bytes 278544 | tf_op jit(solution)/shard_map/psum | solution.py:16
  314.6 1.8 copy.788
  316.5 1.5 copy.884
  318.0 1.5 copy.885
  (296 shorter events, 75.6 us)
Async XLA Ops:
  7.2 16.7 %copy-start.34 = (bf16[2,128,64]{1,2,0:T(8,128)(2,1)S(1)}, bf16[2,128,64]{1,2,0:T(8,128)(2,1)}, u32[]{:S(2)}) copy-start(bf16[2,128,64]{1,2,0:T(8,128)(2,1)} %param.10) | copy-start | bytes 98308
  7.2 25.0 %copy-start.35 = (bf16[2,128,64]{1,2,0:T(8,128)(2,1)S(1)}, bf16[2,128,64]{1,2,0:T(8,128)(2,1)}, u32[]{:S(2)}) copy-start(bf16[2,128,64]{1,2,0:T(8,128)(2,1)} %param.12) | copy-start | bytes 98308
  7.2 13.1 %all-to-all-start.1 = ((bf16[8,128,256]{2,1,0:T(8,128)(2,1)}), bf16[8,128,256]{2,1,0:T(8,128)(2,1)S(1)}, u32[]{:S(2)}, u32[]{:S(2)}) async-start(bf16[8,128,256]{2,1,0:T(8,128)(2,1)} %param.8), calls=%async_computation.1 | async-start | bytes 1048576 | tf_op jit(solution)/shard_map/all_to_all | solution.py:160
  20.3 16.6 %all-to-all-start = ((bf16[8,128,256]{2,1,0:T(8,128)(2,1)}), bf16[8,128,256]{2,1,0:T(8,128)(2,1)S(1)}, u32[]{:S(2)}, u32[]{:S(2)}) async-start(bf16[8,128,256]{2,1,0:T(8,128)(2,1)} %param.9), calls=%async_computation | async-start | bytes 1048576 | tf_op jit(solution)/shard_map/all_to_all | solution.py:161
  23.8 184.8 %reduce-scatter.25.cloned.1.call-start = ((), (), s32[]{:S(2)}) async-start(), calls=%async_computation.14 | async-start | bytes 98304
  32.2 24.1 %copy-start.26 = (bf16[2,256,64]{1,2,0:T(8,128)(2,1)}, bf16[2,256,64]{1,2,0:T(8,128)(2,1)S(1)}, u32[]{:S(2)}) copy-start(bf16[2,256,64]{1,2,0:T(8,128)(2,1)S(1)} %all_gather.18) | copy-start | bytes 196612
  36.8 17.9 %copy-start.31 = (bf16[2,256,64]{1,2,0:T(8,128)(2,1)}, bf16[2,256,64]{1,2,0:T(8,128)(2,1)S(1)}, u32[]{:S(2)}) copy-start(bf16[2,256,64]{1,2,0:T(8,128)(2,1)S(1)} %all_gather.20) | copy-start | bytes 196612
  43.8 4.4 %collective-permute-start.1 = (bf16[8,64,68]{1,0,2:T(8,128)(2,1)S(1)}, bf16[8,64,68]{1,0,2:T(8,128)(2,1)S(1)}, u32[]{:S(2)}, u32[]{:S(2)}) collective-permute-start(bf16[8,64,68]{1,0,2:T(8,128)(2,1)S(1)} %copy.661), channel_id=1, source_target_pairs={{1,0},{4,1},{5,4},{8,5},{9,8},{12,9},{13,12},{3,2},{6,3},{7,6},{10... | collective-permute-start | bytes 208904 | tf_op jit(solution)/shard_map/ppermute | solution.py:33
  45.1 4.0 %collective-permute-start = (bf16[8,64,68]{1,0,2:T(8,128)(2,1)S(1)}, bf16[8,64,68]{1,0,2:T(8,128)(2,1)S(1)}, u32[]{:S(2)}, u32[]{:S(2)}) collective-permute-start(bf16[8,64,68]{1,0,2:T(8,128)(2,1)S(1)} %copy.661), channel_id=1, source_target_pairs={{0,1},{1,4},{4,5},{5,8},{8,9},{9,12},{12,13},{2,3},{3,6},{6,7},{7,... | collective-permute-start | bytes 208904 | tf_op jit(solution)/shard_map/ppermute | solution.py:31
  53.3 1.0 copy-start.6
  54.6 1.4 copy-start.23
  56.1 0.8 copy-start.4
  62.5 4.8 %collective-permute-start.3 = (bf16[8,64,68]{1,0,2:T(8,128)(2,1)S(1)}, bf16[8,64,68]{1,0,2:T(8,128)(2,1)S(1)}, u32[]{:S(2)}, u32[]{:S(2)}) collective-permute-start(bf16[8,64,68]{1,0,2:T(8,128)(2,1)S(1)} %copy.693), channel_id=1, source_target_pairs={{1,0},{4,1},{5,4},{8,5},{9,8},{12,9},{13,12},{3,2},{6,3},{7,6},{10... | collective-permute-start | bytes 208904 | tf_op jit(solution)/shard_map/ppermute | solution.py:33
  63.8 4.5 %collective-permute-start.2 = (bf16[8,64,68]{1,0,2:T(8,128)(2,1)S(1)}, bf16[8,64,68]{1,0,2:T(8,128)(2,1)S(1)}, u32[]{:S(2)}, u32[]{:S(2)}) collective-permute-start(bf16[8,64,68]{1,0,2:T(8,128)(2,1)S(1)} %copy.693), channel_id=1, source_target_pairs={{0,1},{1,4},{4,5},{5,8},{8,9},{9,12},{12,13},{2,3},{3,6},{6,7},{7,... | collective-permute-start | bytes 208904 | tf_op jit(solution)/shard_map/ppermute | solution.py:31
  80.3 5.7 %copy-start.16 = (bf16[1,4,64,256]{3,2,1,0:T(8,128)(2,1)S(1)}, bf16[1,4,64,256]{3,2,1,0:T(8,128)(2,1)}, u32[]{:S(2)}) copy-start(bf16[1,4,64,256]{3,2,1,0:T(8,128)(2,1)} %copy.716) | copy-start | bytes 393220
  84.0 2.3 copy-start.9
  84.0 2.3 copy-start.32
  87.0 0.8 copy-start.5
  88.0 35.4 %copy-start.1 = (bf16[4,64,256]{1,2,0:T(8,128)(2,1)}, bf16[4,64,256]{1,2,0:T(8,128)(2,1)S(1)}, u32[]{:S(2)}) copy-start(bf16[4,64,256]{1,2,0:T(8,128)(2,1)S(1)} %copy.718) | copy-start | bytes 393220
  97.5 10.8 %collective-permute-start.4 = (bf16[8,64,68]{2,0,1:T(8,128)(2,1)}, bf16[8,64,68]{2,0,1:T(8,128)(2,1)}, u32[]{:S(2)}, u32[]{:S(2)}) collective-permute-start(bf16[8,64,68]{2,0,1:T(8,128)(2,1)} %copy.725), channel_id=1, source_target_pairs={{0,1},{1,4},{4,5},{5,8},{8,9},{9,12},{12,13},{2,3},{3,6},{6,7},{7,... | collective-permute-start | bytes 208904 | tf_op jit(solution)/shard_map/ppermute | solution.py:31
  105.5 6.1 %collective-permute-start.5 = (bf16[8,64,68]{2,0,1:T(8,128)(2,1)}, bf16[8,64,68]{2,0,1:T(8,128)(2,1)S(1)}, u32[]{:S(2)}, u32[]{:S(2)}) collective-permute-start(bf16[8,64,68]{2,0,1:T(8,128)(2,1)} %copy.725), channel_id=1, source_target_pairs={{1,0},{4,1},{5,4},{8,5},{9,8},{12,9},{13,12},{3,2},{6,3},{7,6},{10... | collective-permute-start | bytes 208904 | tf_op jit(solution)/shard_map/ppermute | solution.py:33
  108.3 102.7 %reduce-scatter.23.cloned.1.call-start = ((), (), s32[]{:S(2)}) async-start(), calls=%async_computation.13 | async-start | bytes 98304
  123.4 1.8 copy-start.29
  137.8 8.1 %copy-start.14 = (bf16[1,4,64,256]{3,2,1,0:T(8,128)(2,1)S(1)}, bf16[1,4,64,256]{3,2,1,0:T(8,128)(2,1)}, u32[]{:S(2)}) copy-start(bf16[1,4,64,256]{3,2,1,0:T(8,128)(2,1)} %copy.744) | copy-start | bytes 393220
  137.8 8.1 %copy-start.12 = (bf16[1,4,64,256]{3,2,1,0:T(8,128)(2,1)S(1)}, bf16[1,4,64,256]{3,2,1,0:T(8,128)(2,1)}, u32[]{:S(2)}) copy-start(bf16[1,4,64,256]{3,2,1,0:T(8,128)(2,1)} %copy.745) | copy-start | bytes 393220
  141.3 4.7 %copy-start.19 = (bf16[1,4,64,256]{3,2,1,0:T(8,128)(2,1)S(1)}, bf16[1,4,64,256]{3,2,1,0:T(8,128)(2,1)}, u32[]{:S(2)}) copy-start(bf16[1,4,64,256]{3,2,1,0:T(8,128)(2,1)} %copy.747) | copy-start | bytes 393220
  141.3 4.8 %copy-start.17 = (bf16[1,4,64,256]{3,2,1,0:T(8,128)(2,1)S(1)}, bf16[1,4,64,256]{3,2,1,0:T(8,128)(2,1)}, u32[]{:S(2)}) copy-start(bf16[1,4,64,256]{3,2,1,0:T(8,128)(2,1)} %copy.748) | copy-start | bytes 393220
  143.1 2.9 copy-start.21
  143.1 3.0 copy-start.7
  146.0 1.0 copy-start.10
  146.0 1.0 copy-start.27
  146.0 1.4 copy-start.36
  146.5 2.3 copy-start.25
  147.4 1.4 copy-start.24
  147.4 1.6 copy-start.33
  149.5 20.1 %copy-start.2 = (bf16[4,64,256]{2,1,0:T(8,128)(2,1)}, bf16[4,64,256]{2,1,0:T(8,128)(2,1)S(1)}, u32[]{:S(2)}) copy-start(bf16[4,64,256]{2,1,0:T(8,128)(2,1)S(1)} %add_convert_fusion.1) | copy-start | bytes 393220
  149.7 33.3 %copy-start = (bf16[4,64,256]{1,2,0:T(8,128)(2,1)}, bf16[4,64,256]{1,2,0:T(8,128)(2,1)S(1)}, u32[]{:S(2)}) copy-start(bf16[4,64,256]{1,2,0:T(8,128)(2,1)S(1)} %copy.751) | copy-start | bytes 393220
  159.8 9.8 %collective-permute-start.6 = (bf16[8,64,68]{2,0,1:T(8,128)(2,1)}, bf16[8,64,68]{2,0,1:T(8,128)(2,1)}, u32[]{:S(2)}, u32[]{:S(2)}) collective-permute-start(bf16[8,64,68]{2,0,1:T(8,128)(2,1)} %copy.758), channel_id=1, source_target_pairs={{0,1},{1,4},{4,5},{5,8},{8,9},{9,12},{12,13},{2,3},{3,6},{6,7},{7,... | collective-permute-start | bytes 208904 | tf_op jit(solution)/shard_map/ppermute | solution.py:31
  164.8 47.6 %reduce-scatter.21.cloned.1.call-start = ((), (), s32[]{:S(2)}) async-start(), calls=%async_computation.12 | async-start | bytes 98304
  166.8 3.9 %collective-permute-start.7 = (bf16[8,64,68]{2,0,1:T(8,128)(2,1)}, bf16[8,64,68]{2,0,1:T(8,128)(2,1)}, u32[]{:S(2)}, u32[]{:S(2)}) collective-permute-start(bf16[8,64,68]{2,0,1:T(8,128)(2,1)} %copy.758), channel_id=1, source_target_pairs={{1,0},{4,1},{5,4},{8,5},{9,8},{12,9},{13,12},{3,2},{6,3},{7,6},{10... | collective-permute-start | bytes 208904 | tf_op jit(solution)/shard_map/ppermute | solution.py:33
  169.6 49.6 %reduce-scatter.19.cloned.1.call-start = ((), (), s32[]{:S(2)}) async-start(), calls=%async_computation.11 | async-start | bytes 98304
  182.9 1.7 copy-start.30
  197.3 8.1 %copy-start.15 = (bf16[1,4,64,256]{3,2,1,0:T(8,128)(2,1)S(1)}, bf16[1,4,64,256]{3,2,1,0:T(8,128)(2,1)}, u32[]{:S(2)}) copy-start(bf16[1,4,64,256]{3,2,1,0:T(8,128)(2,1)} %copy.777) | copy-start | bytes 393220
  197.3 8.1 %copy-start.3 = (bf16[4,64,256]{2,1,0:T(8,128)(2,1)S(1)}, bf16[4,64,256]{2,1,0:T(8,128)(2,1)}, u32[]{:S(2)}) copy-start(bf16[4,64,256]{2,1,0:T(8,128)(2,1)} %copy-done.2) | copy-start | bytes 393220
  197.3 8.1 %copy-start.13 = (bf16[1,4,64,256]{3,2,1,0:T(8,128)(2,1)S(1)}, bf16[1,4,64,256]{3,2,1,0:T(8,128)(2,1)}, u32[]{:S(2)}) copy-start(bf16[1,4,64,256]{3,2,1,0:T(8,128)(2,1)} %copy.778) | copy-start | bytes 393220
  200.8 4.7 %copy-start.18 = (bf16[1,4,64,256]{3,2,1,0:T(8,128)(2,1)S(1)}, bf16[1,4,64,256]{3,2,1,0:T(8,128)(2,1)}, u32[]{:S(2)}) copy-start(bf16[1,4,64,256]{3,2,1,0:T(8,128)(2,1)} %copy.781) | copy-start | bytes 393220
  202.6 2.9 copy-start.22
  202.6 2.9 copy-start.20
  202.6 3.0 copy-start.8
  207.0 26.5 %reduce-scatter.17.cloned.1.call-start = ((), (), s32[]{:S(2)}) async-start(), calls=%async_computation.10 | async-start | bytes 393216 | tf_op jit(solution)/shard_map/reduce_scatter | solution.py:219
  208.5 38.9 %reduce-scatter.15.cloned.1.call-start = ((), (), s32[]{:S(2)}) async-start(), calls=%async_computation.9 | async-start | bytes 393216 | tf_op jit(solution)/shard_map/reduce_scatter | solution.py:219
  210.9 58.7 %all-reduce.7.cloned.1.call-start = ((), (), s32[]{:S(2)}) async-start(), calls=%async_computation.16 | async-start | bytes 1310720 | tf_op jit(solution)/shard_map/psum | solution.py:16
  212.4 57.2 %copy-start.11 = (bf16[4,256,256]{2,1,0:T(8,128)(2,1)S(1)}, bf16[4,256,256]{2,1,0:T(8,128)(2,1)}, u32[]{:S(2)}) copy-start(bf16[4,256,256]{2,1,0:T(8,128)(2,1)} %get-tuple-element.149) | copy-start | bytes 1572868
  212.4 57.2 %copy-start.28 = (bf16[2,256,64]{1,2,0:T(8,128)(2,1)S(1)}, bf16[2,256,64]{1,2,0:T(8,128)(2,1)}, u32[]{:S(2)}) copy-start(bf16[2,256,64]{1,2,0:T(8,128)(2,1)} %copy-done.26) | copy-start | bytes 196612
  249.2 65.4 %all-reduce.5.cloned.1.call-start = ((), (), s32[]{:S(2)}) async-start(), calls=%async_computation.15 | async-start | bytes 1310720 | tf_op jit(solution)/shard_map/psum | solution.py:16
Sparse Core Ops, SparseCore 0:
  108.4 13.9 reduce-scatter.24
  164.9 9.2 reduce-scatter.22
  177.0 9.8 reduce-scatter.20
  207.1 11.9 reduce-scatter.18
  221.8 11.6 reduce-scatter.16
  235.7 11.6 reduce-scatter.14
  250.5 19.0 all-reduce.6
  272.3 42.3 all-reduce.4
